TPU v7x, 32 devices: a whole 2x2x4 slice. The times are simulated.
32 devices in a mesh: gx: 4 (over y, core), gy: 8 (over z, x).
Axes of the slice: x: 2, y: 2, z: 4, core: 2. Of those that a mesh axis runs over, the one named last changes fastest.
Arguments:
- right_side: float32 [2, 16, 64, 1024], P(None, None, 'gx', 'gy'), may hold values from -12 to 12
- classes: int32 [16, 64, 1024], P(None, 'gx', 'gy'), may hold values from 0 to 15
- sea_mask: int32 [16, 64, 1024], P(None, 'gx', 'gy'), may hold values from 0 to 1, as said below
- kappa_table: float32 [16], replicated, may hold values from 0.002 to 0.2
- cross_table: float32 [16], replicated, may hold values from 0.5 to 4
- vertical_table: float32 [16], replicated, may hold values from 0.05 to 0.5
Outputs:
- solution_field: float32 [2, 16, 64, 1024], P(None, None, 'gx', 'gy')
- residual: float32 [2, 16, 64, 1024], P(None, None, 'gx', 'gy')
Inputs may be any that keep to these rules, and one draw needn't show every extreme that they name: `sea_mask`: land cells (value 0) occur only where both horizontal indices of the cell are even.
All inputs are finite; a program needn't handle non-finite values.
Results may differ from a plain program's by a relative error of at most 0.0055.
Values sent between devices are 32-bit elements; how exact they have to be, the bound alone decides.
A program may use at most 128 MiB of HBM per device.

v0:
```python
import math

import jax
import jax.numpy as jnp
from jax import lax
from jax.sharding import PartitionSpec as P

LEVELS = 3


def with_halo(block, sides, width):
    for axis, dim in sides:
        count = lax.axis_size(axis)
        forward = [(i, i + 1) for i in range(count - 1)]
        backward = [(target, source) for source, target in forward]
        low = lax.ppermute(
            lax.slice_in_dim(block, block.shape[dim] - width, None, axis=dim), axis, forward
        )
        high = lax.ppermute(lax.slice_in_dim(block, 0, width, axis=dim), axis, backward)
        block = jnp.concatenate([low, block, high], axis=dim)
    return block


def cheb_weights(degree, lower_end, upper_end):
    middle = 0.5 * (upper_end + lower_end)
    radius = 0.5 * (upper_end - lower_end)
    return [
        1.0 / (middle + radius * math.cos(math.pi * (2 * index_k + 1) / (2 * degree)))
        for index_k in range(degree)
    ]


def look_up(classes, values_table):
    result = jnp.zeros(classes.shape, jnp.float32)
    for entry in range(values_table.shape[0]):
        result = jnp.where(classes == entry, values_table[entry], result)
    return result


def coarsen_sum(vector):
    shape = vector.shape
    blocks = vector.reshape(shape[:-3] + (shape[-3] // 2, 2, shape[-2] // 2, 2, shape[-1] // 2, 2))
    return jnp.sum(blocks, axis=(-5, -3, -1))


def coarsen_mean(vector):
    return 0.125 * coarsen_sum(vector)


def spread_up(vector):
    return jnp.repeat(jnp.repeat(jnp.repeat(vector, 2, axis=-3), 2, axis=-2), 2, axis=-1)


def build_coeffs(padded_w, vertical, mass_term, factor):
    face_x = factor * jnp.sqrt(padded_w[:, :-1, 1:-1] * padded_w[:, 1:, 1:-1])
    face_y = factor * jnp.sqrt(padded_w[:, 1:-1, :-1] * padded_w[:, 1:-1, 1:])
    face_z = jnp.pad(factor * jnp.sqrt(vertical[:-1] * vertical[1:]), ((1, 1), (0, 0), (0, 0)))
    diagonal = (
        mass_term
        + face_x[:, :-1]
        + face_x[:, 1:]
        + face_y[:, :, :-1]
        + face_y[:, :, 1:]
        + face_z[:-1]
        + face_z[1:]
    )
    return (face_x, face_y, face_z, diagonal)


def apply_operator(vector, coeffs, padded):
    face_x, face_y, face_z, diagonal = coeffs
    padded_z = jnp.pad(vector, ((0, 0), (1, 1), (0, 0), (0, 0)))
    neighbours = face_x[:, :-1] * padded[:, :, :-2, 1:-1] + face_x[:, 1:] * padded[:, :, 2:, 1:-1]
    neighbours = (
        neighbours
        + face_y[:, :, :-1] * padded[:, :, 1:-1, :-2]
        + face_y[:, :, 1:] * padded[:, :, 1:-1, 2:]
    )
    neighbours = neighbours + face_z[:-1] * padded_z[:, :-2] + face_z[1:] * padded_z[:, 2:]
    return diagonal * vector - neighbours


def smooth_pass(approx, source, coeffs, weights, operator):
    for step_index, weight in enumerate(weights):
        if approx is None:
            approx = weight * source / coeffs[3]
        else:
            approx = approx + weight * (source - operator(approx)) / coeffs[3]
    return approx


def pad_sides(vector):
    return with_halo(vector, (("gx", 2), ("gy", 3)), 1)


def pad_material(crosswise):
    return with_halo(crosswise, (("gx", 1), ("gy", 2)), 1)


def cycle_down(source, coeff_list, tier_index):
    coeffs = coeff_list[tier_index]

    def operator(vector):
        return apply_operator(vector, coeffs, pad_sides(vector))

    if tier_index == len(coeff_list) - 1:
        coarse_weights = cheb_weights(4, 0.1, 2.0)
        return smooth_pass(None, source, coeffs, coarse_weights, operator)
    smooth_weights = cheb_weights(2, 0.3, 2.0)
    approx = smooth_pass(None, source, coeffs, smooth_weights, operator)
    defect = source - operator(approx)
    approx = approx + spread_up(cycle_down(coarsen_sum(defect), coeff_list, tier_index + 1))
    return smooth_pass(approx, source, coeffs, smooth_weights, operator)


def shards(right_side, classes, sea_mask, kappa_table, cross_table, vertical_table):
    sea = sea_mask.astype(jnp.float32)
    crosswise = look_up(classes, cross_table) * sea
    vertical = look_up(classes, vertical_table) * sea
    mass_term = look_up(classes, kappa_table) * sea + (1.0 - sea)
    coeff_list = []
    factor = 1.0
    for tier_index in range(LEVELS - 1):
        coeff_list.append(build_coeffs(pad_material(crosswise), vertical, mass_term, factor))
        crosswise = coarsen_mean(crosswise)
        vertical = coarsen_mean(vertical)
        mass_term = coarsen_sum(mass_term)
        factor = 4.0
    coeff_list.append(build_coeffs(pad_material(crosswise), vertical, mass_term, factor))
    direction = cycle_down(cycle_down(right_side, coeff_list, 0), coeff_list, 0)
    local_rz = jnp.sum(right_side * direction, axis=(1, 2, 3))
    first_image = apply_operator(direction, coeff_list[0], pad_sides(direction))
    image = apply_operator(first_image, coeff_list[0], pad_sides(first_image))
    total_rz, total_curve = lax.psum(
        (local_rz, jnp.sum(direction * image, axis=(1, 2, 3))), ("gx", "gy")
    )
    step_length = (total_rz / total_curve)[:, None, None, None]
    return (step_length * direction, right_side - step_length * image)


def solution(mesh):
    return jax.shard_map(
        shards,
        mesh=mesh,
        in_specs=(
            P(None, None, "gx", "gy"),
            P(None, "gx", "gy"),
            P(None, "gx", "gy"),
            P(),
            P(),
            P(),
        ),
        out_specs=(P(None, None, "gx", "gy"), P(None, None, "gx", "gy")),
        check_vma=False,
    )
```

profile of v0, /device:TPU:0, one launch (start us, length us, event | category | flops | bytes accessed | tf_op | source)
XLA Modules:
  0.0 728.8 jit_solution(7004392099396328717)
XLA Ops:
  4.6 11.4 %select_multiply_fusion = (f32[16,16,128]{2,1,0:T(8,128)S(1)}, pred[16,16,128]{2,1,0:T(8,128)(4,1)S(1)}, pred[16,16,128]{2,1,0:T(8,128)(4,1)S(1)}, pred[16,16,12...) fusion(s32[16,16,128]{2,1,0:T(8,128)} %param.8, ...), kind=kLoop, calls=%fused_computation.236 | loop fusion | flops 1114112 | bytes 917568 | tf_op jit(solution)/shard_map/mul | solution.py:119
  15.9 11.1 %select_multiply_fusion.1 = f32[16,16,128]{2,1,0:T(8,128)S(1)} fusion(pred[16,16,128]{2,1,0:T(8,128)(4,1)S(1)} %get-tuple-element.35, pred[16,16,128]{2,1,0:T(8,128)(4,1)S(1)} %get-tuple-element.34, pred[16,16,128]{2,1,0:T(8,128)(4,1)S(1)} %get-tuple-element.33, pred[16,16,128]{2,1,0:T(8,128)(4,1)S(1)} %get-tuple-element.32, ...), kind=kLoop, calls=%fused_computation.237 | loop fusion | flops 589824 | bytes 786496 | tf_op jit(solution)/shard_map/mul | solution.py:118
  30.8 9.7 %reshape.96 = f32[8,2,8,2,64,2]{5,4,3,2,1,0:T(8,128)} reshape(f32[16,16,128]{2,1,0:T(8,128)S(1)} %select_multiply_fusion.1) | data formatting | bytes 262144 | tf_op jit(solution)/shard_map/reshape | solution.py:42
  44.6 5.2 collective-permute-start.12
  56.0 9.7 %reshape.97 = f32[8,2,8,2,64,2]{5,4,3,2,1,0:T(8,128)} reshape(f32[16,16,128]{2,1,0:T(8,128)S(1)} %get-tuple-element.19) | data formatting | bytes 262144 | tf_op jit(solution)/shard_map/reshape | solution.py:42
  65.7 4.1 reduce_sum.111
  81.2 4.6 collective-permute-start.2
  90.4 4.6 collective-permute-done.3
  95.2 10.4 %add_add_fusion = (f32[16,16,128]{2,1,0:T(8,128)S(1)}, f32[16,16,128]{2,1,0:T(8,128)S(1)}) fusion(f32[16,16,129]{2,1,0:T(8,128)S(1)} %fusion.127, f32[16,17,128]{2,1,0:T(8,128)S(1)} %fusion.128, f32[15,16,128]{2,1,0:T(8,128)S(1)} %fusion.129, s32[16,16,128]{2,1,0:T(8,128)S(1)} %copy-done.20, pred[16,16,128]{2,1,0:T(8,128)(4,1)S(1)} %get-tuple-element.35, ...), kind=kLoop, calls=%fused_computation.235 | loop fusion | flops 851968 | bytes 1564736 | tf_op jit(solution)/shard_map/add | solution.py:59
  111.5 4.8 collective-permute-start.6
  117.7 4.4 collective-permute-done.6
  122.1 5.0 collective-permute-done.7
  127.8 4.9 collective-permute-start.8
  132.8 9.7 %reshape.95 = f32[8,2,8,2,64,2]{5,4,3,2,1,0:T(8,128)} reshape(f32[16,16,128]{2,1,0:T(8,128)S(1)} %get-tuple-element.18) | data formatting | bytes 262144 | tf_op jit(solution)/shard_map/reshape | solution.py:42
  142.5 4.1 reduce_sum.109
  149.8 4.1 collective-permute-start.10
  155.5 4.7 collective-permute-done.10
  160.3 6.0 collective-permute-done.11
  166.8 18.1 %reshape.94 = f32[2,8,2,8,2,64,2]{6,5,4,3,2,1,0:T(8,128)} reshape(f32[2,16,16,128]{3,2,1,0:T(8,128)S(1)} %fusion.13) | data formatting | bytes 524288 | tf_op jit(solution)/shard_map/reshape | solution.py:42
  184.9 7.0 reduce_sum.108
  196.2 4.8 collective-permute-start.26
  202.4 7.1 collective-permute-start.18
  212.3 5.0 collective-permute-done.19
  224.0 4.8 collective-permute-start.22
  230.9 4.3 collective-permute-done.23
  252.3 4.2 collective-permute-done.31
  264.4 4.8 collective-permute-start.34
  270.8 4.2 collective-permute-done.35
  287.5 4.2 collective-permute-done.39
  301.0 4.8 collective-permute-start.42
  307.9 4.3 collective-permute-done.43
  325.2 4.3 collective-permute-done.47
  347.3 10.8 %collective-permute-done.50 = f32[2,16,18,1]{3,1,2,0:T(8,128)S(1)} collective-permute-done((f32[2,16,18,1]{3,1,2,0:T(8,128)S(1)}, f32[2,16,18,1]{3,1,2,0:T(8,128)S(1)}, u32[]{:S(2)}, u32[]{:S(2)}) %collective-permute-start.50) | collective-permute-done | bytes 2336 | tf_op jit(solution)/shard_map/ppermute | solution.py:16
  365.6 4.1 collective-permute-start.54
  371.0 11.1 %collective-permute-done.54 = f32[2,16,18,1]{3,1,2,0:T(8,128)S(1)} collective-permute-done((f32[2,16,18,1]{3,1,2,0:T(8,128)S(1)}, f32[2,16,18,1]{3,1,2,0:T(8,128)S(1)}, u32[]{:S(2)}, u32[]{:S(2)}) %collective-permute-start.54) | collective-permute-done | bytes 2336 | tf_op jit(solution)/shard_map/ppermute | solution.py:16
  389.3 4.1 collective-permute-start.58
  394.7 5.0 collective-permute-done.58
  399.7 4.6 collective-permute-done.59
  405.0 4.8 collective-permute-start.60
  413.0 4.1 collective-permute-start.62
  418.4 5.0 collective-permute-done.62
  423.4 5.7 collective-permute-done.63
  429.7 18.1 %reshape.106 = f32[2,8,2,8,2,64,2]{6,5,4,3,2,1,0:T(8,128)} reshape(f32[2,16,16,128]{3,2,1,0:T(8,128)S(1)} %fusion.46) | data formatting | bytes 524288 | tf_op jit(solution)/shard_map/reshape | solution.py:42
  447.8 7.1 reduce_sum.116
  460.9 5.0 collective-permute-start.66
  468.0 6.7 collective-permute-done.67
  481.5 4.8 collective-permute-start.70
  488.3 4.3 collective-permute-done.71
  509.5 4.2 collective-permute-done.75
  526.0 4.2 collective-permute-done.79
  542.6 4.2 collective-permute-done.83
  560.9 4.3 collective-permute-done.87
  578.2 4.3 collective-permute-done.91
  600.4 10.8 %collective-permute-done.94 = f32[2,16,18,1]{3,1,2,0:T(8,128)S(1)} collective-permute-done((f32[2,16,18,1]{3,1,2,0:T(8,128)S(1)}, f32[2,16,18,1]{3,1,2,0:T(8,128)S(1)}, u32[]{:S(2)}, u32[]{:S(2)}) %collective-permute-start.94) | collective-permute-done | bytes 2336 | tf_op jit(solution)/shard_map/ppermute | solution.py:16
  618.6 4.1 collective-permute-start.98
  624.1 11.4 %collective-permute-done.98 = f32[2,16,18,1]{3,1,2,0:T(8,128)S(1)} collective-permute-done((f32[2,16,18,1]{3,1,2,0:T(8,128)S(1)}, f32[2,16,18,1]{3,1,2,0:T(8,128)S(1)}, u32[]{:S(2)}, u32[]{:S(2)}) %collective-permute-start.98) | collective-permute-done | bytes 2336 | tf_op jit(solution)/shard_map/ppermute | solution.py:16
  642.3 4.1 collective-permute-start.102
  647.7 5.0 collective-permute-done.102
  652.7 4.6 collective-permute-done.103
  658.0 4.8 collective-permute-start.104
  666.0 4.1 collective-permute-start.106
  671.4 5.0 collective-permute-done.106
  676.5 5.7 collective-permute-done.107
  683.0 44.5 %all-reduce.27 = (f32[2]{0:T(128)S(1)}, f32[2]{0:T(128)S(1)}) all-reduce(f32[2]{0:T(128)S(1)} %get-tuple-element.11, f32[2]{0:T(128)S(1)} %get-tuple-element.10), channel_id=1, replica_groups=mesh['gx'=4,'gy'=8] {'gx','gy'}, use_global_device_ids=true, to_apply=%region_11.12 | all-reduce | flops 4 | bytes 32 | tf_op jit(solution)/shard_map/psum | solution.py:134
  (439 shorter events, 293.9 us)
Async XLA Ops:
  27.1 53.9 %collective-permute-start = (f32[16,1,128]{2,1,0:T(1,128)S(1)}, f32[16,1,128]{2,1,0:T(1,128)S(1)}, u32[]{:S(2)}, u32[]{:S(2)}) collective-permute-start(f32[16,1,128]{2,1,0:T(1,128)S(1)} %get-tuple-element.102), channel_id=1, source_target_pairs={{0,8},{8,16},{16,24},{1,9},{9,17},{17,25},{2,10},{10,18},{18,26},{... | collective-permute-start | bytes 24584 | tf_op jit(solution)/shard_map/ppermute | solution.py:16
  29.5 51.6 %collective-permute-start.1 = (f32[16,1,128]{2,1,0:T(1,128)S(1)}, f32[16,1,128]{2,1,0:T(1,128)S(1)}, u32[]{:S(2)}, u32[]{:S(2)}) collective-permute-start(f32[16,1,128]{2,1,0:T(1,128)S(1)} %get-tuple-element.103), channel_id=1, source_target_pairs={{8,0},{16,8},{24,16},{9,1},{17,9},{25,17},{10,2},{18,10},{26,18},{... | collective-permute-start | bytes 24584 | tf_op jit(solution)/shard_map/ppermute | solution.py:19
  44.6 29.8 %collective-permute-start.12 = (f32[8,1,64]{2,1,0:T(1,128)S(1)}, f32[8,1,64]{2,1,0:T(1,128)S(1)}, u32[]{:S(2)}, u32[]{:S(2)}) collective-permute-start(f32[8,1,64]{2,1,0:T(1,128)S(1)} %get-tuple-element.173), channel_id=1, source_target_pairs={{0,8},{8,16},{16,24},{1,9},{9,17},{17,25},{2,10},{10,18},{18,26},{... | collective-permute-start | bytes 6152 | tf_op jit(solution)/shard_map/ppermute | solution.py:16
  51.0 21.4 %collective-permute-start.24 = (f32[4,1,32]{2,1,0:T(1,128)S(1)}, f32[4,1,32]{2,1,0:T(1,128)S(1)}, u32[]{:S(2)}, u32[]{:S(2)}) collective-permute-start(f32[4,1,32]{2,1,0:T(1,128)S(1)} %get-tuple-element.196), channel_id=1, source_target_pairs={{0,8},{8,16},{16,24},{1,9},{9,17},{17,25},{2,10},{10,18},{18,26},{... | collective-permute-start | bytes 1544 | tf_op jit(solution)/shard_map/ppermute | solution.py:16
  54.7 19.1 %collective-permute-start.25 = (f32[4,1,32]{2,1,0:T(1,128)S(1)}, f32[4,1,32]{2,1,0:T(1,128)S(1)}, u32[]{:S(2)}, u32[]{:S(2)}) collective-permute-start(f32[4,1,32]{2,1,0:T(1,128)S(1)} %get-tuple-element.197), channel_id=1, source_target_pairs={{8,0},{16,8},{24,16},{9,1},{17,9},{25,17},{10,2},{18,10},{26,18},{... | collective-permute-start | bytes 1544 | tf_op jit(solution)/shard_map/ppermute | solution.py:19
  76.2 56.4 %collective-permute-start.14 = (f32[8,10,1]{2,1,0:T(8,128)S(1)}, f32[8,10,1]{2,1,0:T(8,128)S(1)}, u32[]{:S(2)}, u32[]{:S(2)}) collective-permute-start(f32[8,10,1]{2,1,0:T(8,128)S(1)} %get-tuple-element.157), channel_id=1, source_target_pairs={{0,1},{1,2},{2,3},{3,4},{4,5},{5,6},{6,7},{8,9},{9,10},{10,11},{11... | collective-permute-start | bytes 968 | tf_op jit(solution)/shard_map/ppermute | solution.py:16
  79.7 53.0 %collective-permute-start.15 = (f32[8,10,1]{2,1,0:T(8,128)S(1)}, f32[8,10,1]{2,1,0:T(8,128)S(1)}, u32[]{:S(2)}, u32[]{:S(2)}) collective-permute-start(f32[8,10,1]{2,1,0:T(8,128)S(1)} %get-tuple-element.158), channel_id=1, source_target_pairs={{1,0},{2,1},{3,2},{4,3},{5,4},{6,5},{7,6},{9,8},{10,9},{11,10},{12... | collective-permute-start | bytes 968 | tf_op jit(solution)/shard_map/ppermute | solution.py:19
  81.2 9.2 %collective-permute-start.2 = (f32[16,18,1]{2,1,0:T(8,128)S(1)}, f32[16,18,1]{2,1,0:T(8,128)S(1)}, u32[]{:S(2)}, u32[]{:S(2)}) collective-permute-start(f32[16,18,1]{2,1,0:T(8,128)S(1)} %get-tuple-element.100), channel_id=1, source_target_pairs={{0,1},{1,2},{2,3},{3,4},{4,5},{5,6},{6,7},{8,9},{9,10},{10,11},{11... | collective-permute-start | bytes 3464 | tf_op jit(solution)/shard_map/ppermute | solution.py:16
  85.7 9.3 %collective-permute-start.3 = (f32[16,18,1]{2,1,0:T(8,128)S(1)}, f32[16,18,1]{2,1,0:T(8,128)S(1)}, u32[]{:S(2)}, u32[]{:S(2)}) collective-permute-start(f32[16,18,1]{2,1,0:T(8,128)S(1)} %get-tuple-element.101), channel_id=1, source_target_pairs={{1,0},{2,1},{3,2},{4,3},{5,4},{6,5},{7,6},{9,8},{10,9},{11,10},{12... | collective-permute-start | bytes 3464 | tf_op jit(solution)/shard_map/ppermute | solution.py:19
  111.5 10.6 %collective-permute-start.6 = (f32[2,16,18,1]{3,1,2,0:T(8,128)S(1)}, f32[2,16,18,1]{3,1,2,0:T(8,128)S(1)}, u32[]{:S(2)}, u32[]{:S(2)}) collective-permute-start(f32[2,16,18,1]{3,1,2,0:T(8,128)S(1)} %get-tuple-element.74), channel_id=1, source_target_pairs={{0,1},{1,2},{2,3},{3,4},{4,5},{5,6},{6,7},{8,9},{9,10},{10,11},{11... | collective-permute-start | bytes 6920 | tf_op jit(solution)/shard_map/ppermute | solution.py:16
  116.3 10.8 %collective-permute-start.7 = (f32[2,16,18,1]{3,1,2,0:T(8,128)S(1)}, f32[2,16,18,1]{3,1,2,0:T(8,128)S(1)}, u32[]{:S(2)}, u32[]{:S(2)}) collective-permute-start(f32[2,16,18,1]{3,1,2,0:T(8,128)S(1)} %get-tuple-element.75), channel_id=1, source_target_pairs={{1,0},{2,1},{3,2},{4,3},{5,4},{6,5},{7,6},{9,8},{10,9},{11,10},{12... | collective-permute-start | bytes 6920 | tf_op jit(solution)/shard_map/ppermute | solution.py:19
  127.8 20.1 %collective-permute-start.8 = (f32[2,16,1,128]{3,1,2,0:T(8,128)S(1)}, f32[2,16,1,128]{3,1,2,0:T(8,128)S(1)}, u32[]{:S(2)}, u32[]{:S(2)}) collective-permute-start(f32[2,16,1,128]{3,1,2,0:T(8,128)S(1)} %bitcast.189), channel_id=1, source_target_pairs={{0,8},{8,16},{16,24},{1,9},{9,17},{17,25},{2,10},{10,18},{18,26},{... | collective-permute-start | bytes 49160 | tf_op jit(solution)/shard_map/ppermute | solution.py:16
  149.8 10.5 %collective-permute-start.10 = (f32[2,16,18,1]{3,1,2,0:T(8,128)S(1)}, f32[2,16,18,1]{3,1,2,0:T(8,128)S(1)}, u32[]{:S(2)}, u32[]{:S(2)}) collective-permute-start(f32[2,16,18,1]{3,1,2,0:T(8,128)S(1)} %get-tuple-element.70), channel_id=1, source_target_pairs={{0,1},{1,2},{2,3},{3,4},{4,5},{5,6},{6,7},{8,9},{9,10},{10,11},{11... | collective-permute-start | bytes 6920 | tf_op jit(solution)/shard_map/ppermute | solution.py:16
  153.9 12.3 %collective-permute-start.11 = (f32[2,16,18,1]{3,1,2,0:T(8,128)S(1)}, f32[2,16,18,1]{3,1,2,0:T(8,128)S(1)}, u32[]{:S(2)}, u32[]{:S(2)}) collective-permute-start(f32[2,16,18,1]{3,1,2,0:T(8,128)S(1)} %get-tuple-element.71), channel_id=1, source_target_pairs={{1,0},{2,1},{3,2},{4,3},{5,4},{6,5},{7,6},{9,8},{10,9},{11,10},{12... | collective-permute-start | bytes 6920 | tf_op jit(solution)/shard_map/ppermute | solution.py:19
  192.0 10.3 %collective-permute-start.16 = (f32[2,8,1,64]{3,2,1,0:T(1,128)S(1)}, f32[2,8,1,64]{3,2,1,0:T(1,128)S(1)}, u32[]{:S(2)}, u32[]{:S(2)}) collective-permute-start(f32[2,8,1,64]{3,2,1,0:T(1,128)S(1)} %get-tuple-element.155), channel_id=1, source_target_pairs={{0,8},{8,16},{16,24},{1,9},{9,17},{17,25},{2,10},{10,18},{18,26},{... | collective-permute-start | bytes 12296 | tf_op jit(solution)/shard_map/ppermute | solution.py:16
  194.8 7.5 %collective-permute-start.17 = (f32[2,8,1,64]{3,2,1,0:T(1,128)S(1)}, f32[2,8,1,64]{3,2,1,0:T(1,128)S(1)}, u32[]{:S(2)}, u32[]{:S(2)}) collective-permute-start(f32[2,8,1,64]{3,2,1,0:T(1,128)S(1)} %get-tuple-element.156), channel_id=1, source_target_pairs={{8,0},{16,8},{24,16},{9,1},{17,9},{25,17},{10,2},{18,10},{26,18},{... | collective-permute-start | bytes 12296 | tf_op jit(solution)/shard_map/ppermute | solution.py:19
  196.2 24.4 %collective-permute-start.26 = (f32[4,6,1]{2,1,0:T(8,128)S(1)}, f32[4,6,1]{2,1,0:T(8,128)S(1)}, u32[]{:S(2)}, u32[]{:S(2)}) collective-permute-start(f32[4,6,1]{2,1,0:T(8,128)S(1)} %get-tuple-element.192), channel_id=1, source_target_pairs={{0,1},{1,2},{2,3},{3,4},{4,5},{5,6},{6,7},{8,9},{9,10},{10,11},{11... | collective-permute-start | bytes 296 | tf_op jit(solution)/shard_map/ppermute | solution.py:16
  201.0 19.6 %collective-permute-start.27 = (f32[4,6,1]{2,1,0:T(8,128)S(1)}, f32[4,6,1]{2,1,0:T(8,128)S(1)}, u32[]{:S(2)}, u32[]{:S(2)}) collective-permute-start(f32[4,6,1]{2,1,0:T(8,128)S(1)} %get-tuple-element.193), channel_id=1, source_target_pairs={{1,0},{2,1},{3,2},{4,3},{5,4},{6,5},{7,6},{9,8},{10,9},{11,10},{12... | collective-permute-start | bytes 296 | tf_op jit(solution)/shard_map/ppermute | solution.py:19
  202.4 9.8 %collective-permute-start.18 = (f32[2,8,10,1]{3,1,2,0:T(8,128)S(1)}, f32[2,8,10,1]{3,1,2,0:T(8,128)S(1)}, u32[]{:S(2)}, u32[]{:S(2)}) collective-permute-start(f32[2,8,10,1]{3,1,2,0:T(8,128)S(1)} %get-tuple-element.136), channel_id=1, source_target_pairs={{0,1},{1,2},{2,3},{3,4},{4,5},{5,6},{6,7},{8,9},{9,10},{10,11},{11... | collective-permute-start | bytes 1928 | tf_op jit(solution)/shard_map/ppermute | solution.py:16
  209.6 7.7 %collective-permute-start.19 = (f32[2,8,10,1]{3,1,2,0:T(8,128)S(1)}, f32[2,8,10,1]{3,1,2,0:T(8,128)S(1)}, u32[]{:S(2)}, u32[]{:S(2)}) collective-permute-start(f32[2,8,10,1]{3,1,2,0:T(8,128)S(1)} %get-tuple-element.137), channel_id=1, source_target_pairs={{1,0},{2,1},{3,2},{4,3},{5,4},{6,5},{7,6},{9,8},{10,9},{11,10},{12... | collective-permute-start | bytes 1928 | tf_op jit(solution)/shard_map/ppermute | solution.py:19
  219.2 4.7 collective-permute-start.21
  224.0 6.9 collective-permute-start.22
  228.8 6.3 collective-permute-start.23
  250.7 5.8 collective-permute-start.31
  264.4 6.4 collective-permute-start.34
  269.3 5.8 collective-permute-start.35
  283.0 4.5 collective-permute-start.38
  286.0 5.8 collective-permute-start.39
  301.0 6.9 collective-permute-start.42
  305.8 6.3 collective-permute-start.43
  320.3 4.9 collective-permute-start.46
  323.2 6.3 collective-permute-start.47
  343.1 15.0 %collective-permute-start.50 = (f32[2,16,18,1]{3,1,2,0:T(8,128)S(1)}, f32[2,16,18,1]{3,1,2,0:T(8,128)S(1)}, u32[]{:S(2)}, u32[]{:S(2)}) collective-permute-start(f32[2,16,18,1]{3,1,2,0:T(8,128)S(1)} %get-tuple-element.66), channel_id=1, source_target_pairs={{0,1},{1,2},{2,3},{3,4},{4,5},{5,6},{6,7},{8,9},{9,10},{10,11},{11... | collective-permute-start | bytes 6920 | tf_op jit(solution)/shard_map/ppermute | solution.py:16
  346.0 12.1 %collective-permute-start.51 = (f32[2,16,18,1]{3,1,2,0:T(8,128)S(1)}, f32[2,16,18,1]{3,1,2,0:T(8,128)S(1)}, u32[]{:S(2)}, u32[]{:S(2)}) collective-permute-start(f32[2,16,18,1]{3,1,2,0:T(8,128)S(1)} %get-tuple-element.67), channel_id=1, source_target_pairs={{1,0},{2,1},{3,2},{4,3},{5,4},{6,5},{7,6},{9,8},{10,9},{11,10},{12... | collective-permute-start | bytes 6920 | tf_op jit(solution)/shard_map/ppermute | solution.py:19
  358.8 4.9 collective-permute-start.52
  365.6 16.5 %collective-permute-start.54 = (f32[2,16,18,1]{3,1,2,0:T(8,128)S(1)}, f32[2,16,18,1]{3,1,2,0:T(8,128)S(1)}, u32[]{:S(2)}, u32[]{:S(2)}) collective-permute-start(f32[2,16,18,1]{3,1,2,0:T(8,128)S(1)} %get-tuple-element.62), channel_id=1, source_target_pairs={{0,1},{1,2},{2,3},{3,4},{4,5},{5,6},{6,7},{8,9},{9,10},{10,11},{11... | collective-permute-start | bytes 6920 | tf_op jit(solution)/shard_map/ppermute | solution.py:16
  369.7 12.4 %collective-permute-start.55 = (f32[2,16,18,1]{3,1,2,0:T(8,128)S(1)}, f32[2,16,18,1]{3,1,2,0:T(8,128)S(1)}, u32[]{:S(2)}, u32[]{:S(2)}) collective-permute-start(f32[2,16,18,1]{3,1,2,0:T(8,128)S(1)} %get-tuple-element.63), channel_id=1, source_target_pairs={{1,0},{2,1},{3,2},{4,3},{5,4},{6,5},{7,6},{9,8},{10,9},{11,10},{12... | collective-permute-start | bytes 6920 | tf_op jit(solution)/shard_map/ppermute | solution.py:19
  382.8 4.6 collective-permute-start.56
  389.3 10.4 %collective-permute-start.58 = (f32[2,16,18,1]{3,1,2,0:T(8,128)S(1)}, f32[2,16,18,1]{3,1,2,0:T(8,128)S(1)}, u32[]{:S(2)}, u32[]{:S(2)}) collective-permute-start(f32[2,16,18,1]{3,1,2,0:T(8,128)S(1)} %get-tuple-element.58), channel_id=1, source_target_pairs={{0,1},{1,2},{2,3},{3,4},{4,5},{5,6},{6,7},{8,9},{9,10},{10,11},{11... | collective-permute-start | bytes 6920 | tf_op jit(solution)/shard_map/ppermute | solution.py:16
  393.4 10.9 %collective-permute-start.59 = (f32[2,16,18,1]{3,1,2,0:T(8,128)S(1)}, f32[2,16,18,1]{3,1,2,0:T(8,128)S(1)}, u32[]{:S(2)}, u32[]{:S(2)}) collective-permute-start(f32[2,16,18,1]{3,1,2,0:T(8,128)S(1)} %get-tuple-element.59), channel_id=1, source_target_pairs={{1,0},{2,1},{3,2},{4,3},{5,4},{6,5},{7,6},{9,8},{10,9},{11,10},{12... | collective-permute-start | bytes 6920 | tf_op jit(solution)/shard_map/ppermute | solution.py:19
  405.0 6.1 collective-permute-start.60
  413.0 10.5 %collective-permute-start.62 = (f32[2,16,18,1]{3,1,2,0:T(8,128)S(1)}, f32[2,16,18,1]{3,1,2,0:T(8,128)S(1)}, u32[]{:S(2)}, u32[]{:S(2)}) collective-permute-start(f32[2,16,18,1]{3,1,2,0:T(8,128)S(1)} %get-tuple-element.54), channel_id=1, source_target_pairs={{0,1},{1,2},{2,3},{3,4},{4,5},{5,6},{6,7},{8,9},{9,10},{10,11},{11... | collective-permute-start | bytes 6920 | tf_op jit(solution)/shard_map/ppermute | solution.py:16
  417.1 12.0 %collective-permute-start.63 = (f32[2,16,18,1]{3,1,2,0:T(8,128)S(1)}, f32[2,16,18,1]{3,1,2,0:T(8,128)S(1)}, u32[]{:S(2)}, u32[]{:S(2)}) collective-permute-start(f32[2,16,18,1]{3,1,2,0:T(8,128)S(1)} %get-tuple-element.55), channel_id=1, source_target_pairs={{1,0},{2,1},{3,2},{4,3},{5,4},{6,5},{7,6},{9,8},{10,9},{11,10},{12... | collective-permute-start | bytes 6920 | tf_op jit(solution)/shard_map/ppermute | solution.py:19
  460.9 7.1 collective-permute-start.66
  465.9 8.7 %collective-permute-start.67 = (f32[2,8,10,1]{3,1,2,0:T(8,128)S(1)}, f32[2,8,10,1]{3,1,2,0:T(8,128)S(1)}, u32[]{:S(2)}, u32[]{:S(2)}) collective-permute-start(f32[2,8,10,1]{3,1,2,0:T(8,128)S(1)} %get-tuple-element.121), channel_id=1, source_target_pairs={{1,0},{2,1},{3,2},{4,3},{5,4},{6,5},{7,6},{9,8},{10,9},{11,10},{12... | collective-permute-start | bytes 1928 | tf_op jit(solution)/shard_map/ppermute | solution.py:19
  481.5 6.9 collective-permute-start.70
  486.3 6.3 collective-permute-start.71
  507.9 5.8 collective-permute-start.75
  524.4 5.8 collective-permute-start.79
  541.0 5.8 collective-permute-start.83
  556.0 4.9 collective-permute-start.86
  558.9 6.3 collective-permute-start.87
  573.4 4.9 collective-permute-start.90
  576.2 6.3 collective-permute-start.91
  596.2 15.0 %collective-permute-start.94 = (f32[2,16,18,1]{3,1,2,0:T(8,128)S(1)}, f32[2,16,18,1]{3,1,2,0:T(8,128)S(1)}, u32[]{:S(2)}, u32[]{:S(2)}) collective-permute-start(f32[2,16,18,1]{3,1,2,0:T(8,128)S(1)} %get-tuple-element.50), channel_id=1, source_target_pairs={{0,1},{1,2},{2,3},{3,4},{4,5},{5,6},{6,7},{8,9},{9,10},{10,11},{11... | collective-permute-start | bytes 6920 | tf_op jit(solution)/shard_map/ppermute | solution.py:16
  599.1 12.1 %collective-permute-start.95 = (f32[2,16,18,1]{3,1,2,0:T(8,128)S(1)}, f32[2,16,18,1]{3,1,2,0:T(8,128)S(1)}, u32[]{:S(2)}, u32[]{:S(2)}) collective-permute-start(f32[2,16,18,1]{3,1,2,0:T(8,128)S(1)} %get-tuple-element.51), channel_id=1, source_target_pairs={{1,0},{2,1},{3,2},{4,3},{5,4},{6,5},{7,6},{9,8},{10,9},{11,10},{12... | collective-permute-start | bytes 6920 | tf_op jit(solution)/shard_map/ppermute | solution.py:19
  611.8 4.9 collective-permute-start.96
  618.6 16.8 %collective-permute-start.98 = (f32[2,16,18,1]{3,1,2,0:T(8,128)S(1)}, f32[2,16,18,1]{3,1,2,0:T(8,128)S(1)}, u32[]{:S(2)}, u32[]{:S(2)}) collective-permute-start(f32[2,16,18,1]{3,1,2,0:T(8,128)S(1)} %get-tuple-element.46), channel_id=1, source_target_pairs={{0,1},{1,2},{2,3},{3,4},{4,5},{5,6},{6,7},{8,9},{9,10},{10,11},{11... | collective-permute-start | bytes 6920 | tf_op jit(solution)/shard_map/ppermute | solution.py:16
  622.8 12.7 %collective-permute-start.99 = (f32[2,16,18,1]{3,1,2,0:T(8,128)S(1)}, f32[2,16,18,1]{3,1,2,0:T(8,128)S(1)}, u32[]{:S(2)}, u32[]{:S(2)}) collective-permute-start(f32[2,16,18,1]{3,1,2,0:T(8,128)S(1)} %get-tuple-element.47), channel_id=1, source_target_pairs={{1,0},{2,1},{3,2},{4,3},{5,4},{6,5},{7,6},{9,8},{10,9},{11,10},{12... | collective-permute-start | bytes 6920 | tf_op jit(solution)/shard_map/ppermute | solution.py:19
  642.3 10.4 %collective-permute-start.102 = (f32[2,16,18,1]{3,1,2,0:T(8,128)S(1)}, f32[2,16,18,1]{3,1,2,0:T(8,128)S(1)}, u32[]{:S(2)}, u32[]{:S(2)}) collective-permute-start(f32[2,16,18,1]{3,1,2,0:T(8,128)S(1)} %get-tuple-element.42), channel_id=1, source_target_pairs={{0,1},{1,2},{2,3},{3,4},{4,5},{5,6},{6,7},{8,9},{9,10},{10,11},{11... | collective-permute-start | bytes 6920 | tf_op jit(solution)/shard_map/ppermute | solution.py:16
  646.4 10.9 %collective-permute-start.103 = (f32[2,16,18,1]{3,1,2,0:T(8,128)S(1)}, f32[2,16,18,1]{3,1,2,0:T(8,128)S(1)}, u32[]{:S(2)}, u32[]{:S(2)}) collective-permute-start(f32[2,16,18,1]{3,1,2,0:T(8,128)S(1)} %get-tuple-element.43), channel_id=1, source_target_pairs={{1,0},{2,1},{3,2},{4,3},{5,4},{6,5},{7,6},{9,8},{10,9},{11,10},{12... | collective-permute-start | bytes 6920 | tf_op jit(solution)/shard_map/ppermute | solution.py:19
  658.0 6.1 collective-permute-start.104
  666.0 10.5 %collective-permute-start.106 = (f32[2,16,18,1]{3,1,2,0:T(8,128)S(1)}, f32[2,16,18,1]{3,1,2,0:T(8,128)S(1)}, u32[]{:S(2)}, u32[]{:S(2)}) collective-permute-start(f32[2,16,18,1]{3,1,2,0:T(8,128)S(1)} %get-tuple-element.38), channel_id=1, source_target_pairs={{0,1},{1,2},{2,3},{3,4},{4,5},{5,6},{6,7},{8,9},{9,10},{10,11},{11... | collective-permute-start | bytes 6920 | tf_op jit(solution)/shard_map/ppermute | solution.py:16
  670.1 12.0 %collective-permute-start.107 = (f32[2,16,18,1]{3,1,2,0:T(8,128)S(1)}, f32[2,16,18,1]{3,1,2,0:T(8,128)S(1)}, u32[]{:S(2)}, u32[]{:S(2)}) collective-permute-start(f32[2,16,18,1]{3,1,2,0:T(8,128)S(1)} %get-tuple-element.39), channel_id=1, source_target_pairs={{1,0},{2,1},{3,2},{4,3},{5,4},{6,5},{7,6},{9,8},{10,9},{11,10},{12... | collective-permute-start | bytes 6920 | tf_op jit(solution)/shard_map/ppermute | solution.py:19
  (72 other events, 1282.8 us)
where the time goes:
time: 742 us; the launch traced here: 729 us
  starting transfers between devices  263 us (35%)
  waiting for transfers between devices  236 us (32%)
  local copies, waits for them, and re-layouts  93.2 us (13%)
  other arithmetic  88.4 us (12%)
  blocking collectives  44.5 us (6%)
    ppermute x54, starting transfers between devices, with_halo(): lax.ppermute(lax.slice_in_dim(block, block.shape[dim] - width, None, axis...  193 us
    ppermute x54, waiting for transfers between devices, with_halo(): lax.ppermute(lax.slice_in_dim(block, 0, width, axis=dim), axis, backward)  152 us
    ppermute x54, waiting for transfers between devices, with_halo(): lax.ppermute(lax.slice_in_dim(block, block.shape[dim] - width, None, axis...  83.8 us
    reshape x8, local copies, waits for them, and re-layouts, coarsen_sum(): vector.reshape(shape[:-3] + (shape[-3] // 2, 2, shape[-2] // 2, 2, shape[...  72.4 us
    ppermute x54, starting transfers between devices, with_halo(): lax.ppermute(lax.slice_in_dim(block, 0, width, axis=dim), axis, backward)  70.2 us
    psum x1, blocking collectives, shards(): lax.psum((local_rz, jnp.sum(direction * image, axis=(1, 2, 3))), ('gx', '...  44.5 us
    reduce_sum x10, other arithmetic, coarsen_sum(): return jnp.sum(blocks, axis=(-5, -3, -1))  28.4 us
  transfers between devices with their start and end apart: 108, of which 70 were waited for; matrix products, arithmetic and copies ran while one was open for 8% of the time, Pallas kernels for 0%

commit v1 on v0

v1 whole, which is shorter than its diff:
```python
import functools
import math

import jax
import jax.numpy as jnp
from jax import lax
from jax.experimental import pallas as pl
from jax.experimental.pallas import tpu as pltpu
from jax.sharding import PartitionSpec as P

MESH = pl.DeviceIdType.MESH
ROWS, LANES = 16, 128
WIDE = 2 * LANES
WAYS = ((-1, 0), (1, 0), (0, -1), (0, 1), (-1, -1), (1, -1), (-1, 1), (1, 1))


def cheb_weights(degree, lower_end, upper_end):
    middle = 0.5 * (upper_end + lower_end)
    radius = 0.5 * (upper_end - lower_end)
    return [
        1.0 / (middle + radius * math.cos(math.pi * (2 * index_k + 1) / (2 * degree)))
        for index_k in range(degree)
    ]


def turn(value, shift, axis):
    size = value.shape[axis]
    shift = shift % size
    return value if shift == 0 else pltpu.roll(value, shift, axis)


def pair_sum(value, step):
    for axis in (value.ndim - 2, value.ndim - 1):
        place = lax.broadcasted_iota(jnp.int32, value.shape, axis)
        first = (place // step) % 2 == 0
        value = value + jnp.where(first, turn(value, -step, axis), turn(value, step, axis))
    return value


def loop(count, body):
    def run(index, carry):
        body(index)
        return carry

    lax.fori_loop(0, count, run, 0)


class Level:
    def __init__(self, refs, depth, step, factor):
        self.w, self.u, self.k, self.fxm, self.fxp, self.fym, self.fyp, self.fz, self.d, self.inv = refs
        self.depth, self.step, self.factor = depth, step, factor

    def build(self, diagonal_known=False):
        step, factor = self.step, self.factor

        def body(z):
            w = self.w[z + 1]
            fxp = factor * jnp.sqrt(w * turn(w, -step, 0))
            fyp = factor * jnp.sqrt(w * turn(w, -step, 1))
            fxm = turn(fxp, step, 0)
            fym = turn(fyp, step, 1)
            fzm = factor * jnp.sqrt(self.u[z] * self.u[z + 1])
            fzp = factor * jnp.sqrt(self.u[z + 1] * self.u[z + 2])
            d = self.k[z + 1]
            if not diagonal_known:
                d = d + fxm + fxp + fym + fyp + fzm + fzp
            self.fxm[z], self.fxp[z], self.fym[z], self.fyp[z] = fxm, fxp, fym, fyp
            self.fz[z] = fzm
            self.fz[z + 1] = fzp
            self.d[z] = d
            self.inv[z] = jnp.where(d > 0.0, 1.0 / jnp.where(d > 0.0, d, 1.0), 0.0)

        loop(self.depth, body)

    def operator(self, v, z):
        x = v[:, z + 1]
        step = self.step
        total = self.fxm[z] * turn(x, step, 1) + self.fxp[z] * turn(x, -step, 1)
        total = total + self.fym[z] * turn(x, step, 2) + self.fyp[z] * turn(x, -step, 2)
        total = total + self.fz[z] * v[:, z] + self.fz[z + 1] * v[:, z + 2]
        return self.d[z] * x - total

    def start(self, out, r, weight):
        def body(z):
            out[:, z + 1] = weight * r[:, z + 1] * self.inv[z]

        loop(self.depth, body)

    def smooth(self, out, v, r, weight):
        def body(z):
            out[:, z + 1] = v[:, z + 1] + weight * (r[:, z + 1] - self.operator(v, z)) * self.inv[z]

        loop(self.depth, body)


class Exchange:
    def __init__(self, refs, send_sem, recv_sem, row, width, depth):
        self.left, self.right, self.rows_in, self.from_right, self.from_left = refs
        self.send_sem, self.recv_sem, self.row = send_sem, recv_sem, row
        self.width, self.depth = width, depth

    def clear(self):
        for ref in (self.rows_in, self.from_right, self.from_left):
            ref[...] = jnp.zeros(ref.shape, jnp.float32)

    def pack(self, source):
        width, groups = self.width, LANES // self.width
        shape = self.left.shape
        group = lax.broadcasted_iota(jnp.int32, shape, 2) // width
        left = jnp.zeros(shape, jnp.float32)
        right = jnp.zeros(shape, jnp.float32)
        for z in range(self.depth):
            moved = turn(source[:, z], width * z, 2)
            left = jnp.where(group == z, moved, left)
            right = jnp.where(group == (z - 1) % groups, moved, right)
        self.left[...] = left
        self.right[...] = right

    def copies(self, source):
        h = self.width
        low, high = pl.ds(0, h), pl.ds(ROWS - h, h)
        near, far = pl.ds(ROWS, h), pl.ds(ROWS + h, h)
        whole = pl.ds(0, ROWS)
        ends = (
            (source.at[:, :, low], self.rows_in.at[:, :, pl.ds(0, h)]),
            (source.at[:, :, high], self.rows_in.at[:, :, pl.ds(h, h)]),
            (self.left, self.from_right.at[:, whole]),
            (self.right, self.from_left.at[:, whole]),
            (self.left.at[:, low], self.from_right.at[:, near]),
            (self.left.at[:, high], self.from_right.at[:, far]),
            (self.right.at[:, low], self.from_left.at[:, near]),
            (self.right.at[:, high], self.from_left.at[:, far]),
        )
        gx, gy = lax.axis_index("gx"), lax.axis_index("gy")
        nx, ny = lax.axis_size("gx"), lax.axis_size("gy")
        for way, ((dx, dy), (src, dst)) in enumerate(zip(WAYS, ends)):
            copy = pltpu.make_async_remote_copy(
                src_ref=src,
                dst_ref=dst,
                send_sem=self.send_sem.at[self.row, way],
                recv_sem=self.recv_sem.at[self.row, way],
                device_id=(lax.rem(gx + dx + nx, nx), lax.rem(gy + dy + ny, ny)),
                device_id_type=MESH,
            )
            yield copy, exists(gx, nx, dx) & exists(gy, ny, dy), exists(gx, nx, -dx) & exists(gy, ny, -dy)

    def begin(self, source):
        self.pack(source)
        for copy, sends, _ in self.copies(source):
            pl.when(sends)(copy.start)

    def finish(self, source):
        for copy, sends, receives in self.copies(source):
            pl.when(sends)(copy.wait_send)
            pl.when(receives)(copy.wait_recv)

    def unpack(self, out, source, count):
        h = self.width
        lane = lax.broadcasted_iota(jnp.int32, self.from_right.shape, 2)
        from_right, from_left = self.from_right[...], self.from_left[...]
        for z in range(self.depth):
            side = jnp.where(
                lane < h,
                turn(from_right, -h * z, 2),
                jnp.where(lane >= LANES - h, turn(from_left, -h * z, 2), 0.0),
            )
            for item in range(count):
                target = out[item] if isinstance(out, tuple) else out.at[item]
                if source is not None:
                    target[z + 1, 0:ROWS, 0:LANES] = source[item, z]
                target[z + 1, ROWS : ROWS + 2 * h, 0:LANES] = self.rows_in[item, z]
                target[z + 1, :, LANES:WIDE] = side[item]


def exists(index, count, step):
    if step < 0:
        return index > 0
    if step > 0:
        return index < count - 1
    return index >= 0


def greet():
    gx, gy = lax.axis_index("gx"), lax.axis_index("gy")
    nx, ny = lax.axis_size("gx"), lax.axis_size("gy")
    barrier = pltpu.get_barrier_semaphore()
    for step in range(1, nx):
        pl.semaphore_signal(barrier, inc=1, device_id=(lax.rem(gx + step, nx), gy), device_id_type=MESH)
    for step in range(1, ny):
        pl.semaphore_signal(barrier, inc=1, device_id=(gx, lax.rem(gy + step, ny)), device_id_type=MESH)
    for dx, dy in WAYS[4:]:
        there = (lax.rem(gx + dx + nx, nx), lax.rem(gy + dy + ny, ny))

        @pl.when(exists(gx, nx, dx) & exists(gy, ny, dy))
        def _():
            pl.semaphore_signal(barrier, inc=1, device_id=there, device_id_type=MESH)

    beside_x = (gx > 0).astype(jnp.int32) + (gx < nx - 1).astype(jnp.int32)
    beside_y = (gy > 0).astype(jnp.int32) + (gy < ny - 1).astype(jnp.int32)
    pl.semaphore_wait(barrier, nx - 1 + ny - 1 + beside_x * beside_y)


def sum_over(axis, mine, slots, send_sem, recv_sem):
    count = lax.axis_size(axis)
    me = lax.axis_index(axis)
    copies = []
    for step in range(1, count):
        copy = pltpu.make_async_remote_copy(
            src_ref=mine,
            dst_ref=slots.at[step - 1],
            send_sem=send_sem.at[step - 1],
            recv_sem=recv_sem.at[step - 1],
            device_id={axis: lax.rem(me + step, count)},
            device_id_type=MESH,
        )
        copy.start()
        copies.append(copy)
    total = mine[...]
    for step, copy in enumerate(copies):
        copy.wait()
        total = total + slots[step]
    return total


def kernel(depth, entries, *refs):
    refs = list(refs)

    def take(count):
        got = tuple(refs[:count])
        del refs[:count]
        return got

    right_side, classes, sea_mask, kappa, cross, vertical = take(6)
    direction_out, image_out, alpha_out = take(3)
    level0 = Level(take(10), depth, 1, 1.0)
    level1 = Level(take(10), depth // 2, 2, 4.0)
    level2 = Level(take(10), depth // 4, 4, 4.0)
    inner2 = Level(take(10), depth // 4, 4, 4.0)
    r_first, r_second, xa, xb = take(4)
    r1, ya, yb = take(3)
    r2, za, zb = take(3)
    material, material2, = take(2)
    r2_own = take(2)
    y_own = take(2)
    x_own = take(2)
    names = ("r", "mat", "mat2", "e2a", "e2b", "ya", "yb", "e4a", "e4b")
    boxes = [take(5) for _ in names]
    part_x, part_y, slots_x, slots_y = take(4)
    send_sem, recv_sem, sx_send, sx_recv, sy_send, sy_recv = take(6)
    widths = (8, 8, 16, 16, 16, 8, 8, 8, 8)
    depths = (depth, depth, depth // 4, depth // 4, depth // 4, depth // 2, depth // 2, depth, depth)
    ex = {
        name: Exchange(box, send_sem, recv_sem, row, width, size)
        for row, (name, box, width, size) in enumerate(zip(names, boxes, widths, depths))
    }
    for exchange in ex.values():
        exchange.clear()
    greet()

    ex["r"].begin(right_side)

    def look_up(z):
        cls = classes[z]
        sea = sea_mask[z].astype(jnp.float32)
        w = jnp.zeros(cls.shape, jnp.float32)
        u, k = w, w
        for entry in range(entries):
            here = cls == entry
            w = jnp.where(here, cross[entry], w)
            u = jnp.where(here, vertical[entry], u)
            k = jnp.where(here, kappa[entry], k)
        material[0, z] = w * sea
        material[1, z] = u * sea
        material[2, z] = k * sea + (1.0 - sea)

    loop(depth, look_up)
    ex["mat"].begin(material)
    for ref in (r_first, r_second, xa, xb, r1, ya, yb, r2, za, zb):
        last = ref.shape[1] - 1
        ref[:, 0] = jnp.zeros(ref.shape[:1] + ref.shape[2:], jnp.float32)
        ref[:, last] = jnp.zeros(ref.shape[:1] + ref.shape[2:], jnp.float32)
    for level in (level0, level1, level2, inner2):
        level.u[0] = jnp.zeros(level.u.shape[1:], jnp.float32)
        level.u[level.depth + 1] = jnp.zeros(level.u.shape[1:], jnp.float32)
    ex["r"].finish(right_side)
    ex["r"].unpack(r_first, right_side, 2)
    ex["mat"].finish(material)
    ex["mat"].unpack((level0.w, level0.u, level0.k), material, 3)

    def coarsen_material(fine, coarse, step):
        def body(z):
            for src, dst, factor in (
                (fine.w, coarse.w, 0.125),
                (fine.u, coarse.u, 0.125),
                (fine.k, coarse.k, 1.0),
            ):
                dst[z + 1] = factor * pair_sum(src[2 * z + 1] + src[2 * z + 2], step)

        loop(coarse.depth, body)

    coarsen_material(level0, level1, 1)
    coarsen_material(level1, inner2, 2)
    inner2.build()

    def own_material2(z):
        material2[0, z] = inner2.w[z + 1, 0:ROWS, 0:LANES]
        material2[1, z] = inner2.u[z + 1, 0:ROWS, 0:LANES]
        material2[2, z] = inner2.d[z, 0:ROWS, 0:LANES]

    loop(level2.depth, own_material2)
    ex["mat2"].begin(material2)
    level0.build()
    level1.build()

    fine_w = cheb_weights(2, 0.3, 2.0)
    coarse_w = cheb_weights(4, 0.1, 2.0)

    def cycle(r, out, turn_no):
        level0.start(xa, r, fine_w[0])
        level0.smooth(xb, xa, r, fine_w[1])

        def down0(z):
            q = r[:, 2 * z + 1] - level0.operator(xb, 2 * z)
            q = q + (r[:, 2 * z + 2] - level0.operator(xb, 2 * z + 1))
            q = pair_sum(q, 1)
            r1[:, z + 1] = q
            ya[:, z + 1] = fine_w[0] * q * level1.inv[z]

        loop(level1.depth, down0)
        level1.smooth(yb, ya, r1, fine_w[1])
        own2 = r2_own[turn_no]

        def down1(z):
            q = r1[:, 2 * z + 1] - level1.operator(yb, 2 * z)
            q = q + (r1[:, 2 * z + 2] - level1.operator(yb, 2 * z + 1))
            own2[:, z] = pair_sum(q, 2)[:, 0:ROWS, 0:LANES]

        loop(level2.depth, down1)
        e2 = ex[("e2a", "e2b")[turn_no]]
        e2.begin(own2)
        own1 = y_own[turn_no]

        def keep(z):
            own1[:, z] = yb[:, z + 1, 0:ROWS, 0:LANES]

        loop(level1.depth, keep)
        e1 = ex[("ya", "yb")[turn_no]]
        e1.begin(own1)
        if turn_no == 0:
            ex["mat2"].finish(material2)
            ex["mat2"].unpack((level2.w, level2.u, level2.k), material2, 3)
            level2.build(True)
        e2.finish(own2)
        e2.unpack(r2, own2, 2)
        level2.start(za, r2, coarse_w[0])
        level2.smooth(zb, za, r2, coarse_w[1])
        level2.smooth(za, zb, r2, coarse_w[2])
        level2.smooth(zb, za, r2, coarse_w[3])
        e1.finish(own1)
        e1.unpack(yb, None, 2)

        def up1(z):
            add = jnp.concatenate([zb[:, z + 1, 0:24], zb[:, z + 1, 40:48]], axis=1)
            ya[:, 2 * z + 1] = yb[:, 2 * z + 1] + add
            ya[:, 2 * z + 2] = yb[:, 2 * z + 2] + add

        loop(level2.depth, up1)
        level1.smooth(yb, ya, r1, fine_w[0])
        level1.smooth(ya, yb, r1, fine_w[1])
        own = x_own[turn_no]

        def up0(z):
            add = ya[:, z + 1, 0:ROWS, 0:LANES]
            own[:, 2 * z] = xb[:, 2 * z + 1, 0:ROWS, 0:LANES] + add
            own[:, 2 * z + 1] = xb[:, 2 * z + 2, 0:ROWS, 0:LANES] + add

        loop(level1.depth, up0)
        e4 = ex[("e4a", "e4b")[turn_no]]
        e4.begin(own)
        e4.finish(own)
        e4.unpack(xa, own, 2)
        level0.smooth(xb, xa, r, fine_w[0])
        level0.smooth(out, xb, r, fine_w[1])

    cycle(r_first, r_second, 0)
    cycle(r_second, r_first, 1)

    def first_image(z):
        xb[:, z + 1] = level0.operator(r_first, z)

    loop(depth, first_image)

    def second_image(z, sums):
        image = level0.operator(xb, z)[:, 0:ROWS, 0:LANES]
        direction = r_first[:, z + 1, 0:ROWS, 0:LANES]
        direction_out[:, z] = direction
        image_out[:, z] = image
        return sums[0] + right_side[:, z] * direction, sums[1] + direction * image

    zero = jnp.zeros((2, ROWS, LANES), jnp.float32)
    rz, curve = lax.fori_loop(0, depth, second_image, (zero, zero))
    part_x[0:2] = rz[:, 0:8] + rz[:, 8:16]
    part_x[2:4] = curve[:, 0:8] + curve[:, 8:16]
    part_y[...] = sum_over("gx", part_x, slots_x, sx_send, sx_recv)
    total = sum_over("gy", part_y, slots_y, sy_send, sy_recv)
    total = jnp.sum(total, axis=2, keepdims=True)
    total = jnp.sum(total, axis=1, keepdims=True)
    alpha_out[...] = jnp.broadcast_to(total[0:2] / total[2:4], alpha_out.shape)


def shards(right_side, classes, sea_mask, kappa_table, cross_table, vertical_table):
    nx, ny = lax.axis_size("gx"), lax.axis_size("gy")
    depth = classes.shape[0]

    def buf(*shape):
        return pltpu.VMEM(shape, jnp.float32)

    def level(size, rows):
        pad, one, face = buf(size + 2, rows, WIDE), buf(size, rows, WIDE), buf(size + 1, rows, WIDE)
        return [pad, pad, pad, one, one, one, one, face, one, one]

    def box(items, size, width):
        sides = buf(items, ROWS + 2 * width, LANES)
        pack = buf(items, ROWS, LANES)
        return [pack, pack, buf(items, size, 2 * width, LANES), sides, sides]

    d0, d1, d2 = depth, depth // 2, depth // 4
    scratch = level(d0, 32) + level(d1, 32) + level(d2, 48) + level(d2, 32)
    scratch += [buf(2, d0 + 2, 32, WIDE)] * 4
    scratch += [buf(2, d1 + 2, 32, WIDE)] * 3
    scratch += [buf(2, d2 + 2, 48, WIDE)] * 3
    scratch += [buf(3, d0, ROWS, LANES), buf(3, d2, ROWS, LANES)]
    scratch += [buf(2, d2, ROWS, LANES)] * 2 + [buf(2, d1, ROWS, LANES)] * 2 + [buf(2, d0, ROWS, LANES)] * 2
    scratch += box(2, d0, 8) + box(3, d0, 8) + box(3, d2, 16) + box(2, d2, 16) + box(2, d2, 16)
    scratch += box(2, d1, 8) + box(2, d1, 8) + box(2, d0, 8) + box(2, d0, 8)
    scratch += [buf(4, 8, LANES)] * 2 + [buf(nx - 1, 4, 8, LANES), buf(ny - 1, 4, 8, LANES)]
    dma = pltpu.SemaphoreType.DMA
    scratch += [dma((9, 8)), dma((9, 8)), dma((nx - 1,)), dma((nx - 1,)), dma((ny - 1,)), dma((ny - 1,))]
    vmem = pl.BlockSpec(memory_space=pltpu.VMEM)
    smem = pl.BlockSpec(memory_space=pltpu.SMEM)
    field = jax.ShapeDtypeStruct(right_side.shape, jnp.float32)
    direction, image, alpha = pl.pallas_call(
        functools.partial(kernel, depth, kappa_table.shape[0]),
        out_shape=(field, field, jax.ShapeDtypeStruct((2, 8, LANES), jnp.float32)),
        in_specs=[vmem, vmem, vmem, smem, smem, smem],
        out_specs=(vmem, vmem, vmem),
        scratch_shapes=scratch,
        compiler_params=pltpu.CompilerParams(
            collective_id=0, has_side_effects=True, vmem_limit_bytes=48 * 1024 * 1024
        ),
    )(right_side, classes, sea_mask, kappa_table, cross_table, vertical_table)
    alpha = alpha[:, 0:1, 0:1, None]
    return alpha * direction, right_side - alpha * image


def solution(mesh):
    return jax.shard_map(
        shards,
        mesh=mesh,
        in_specs=(
            P(None, None, "gx", "gy"),
            P(None, "gx", "gy"),
            P(None, "gx", "gy"),
            P(),
            P(),
            P(),
        ),
        out_specs=(P(None, None, "gx", "gy"), P(None, None, "gx", "gy")),
        check_vma=False,
    )
```

time: 742 us -> 86.1 us (0.12); the launches traced: 729 us -> 85.9 us
  starting transfers between devices: 263 us -> 0 us
  waiting for transfers between devices: 236 us -> 0 us
  local copies, waits for them, and re-layouts: 93.2 us -> 4.82 us
  other arithmetic: 88.4 us -> 0.91 us
  Pallas kernels: 0 us -> 79.5 us
  blocking collectives: 44.5 us -> 0 us
    ppermute x108 -> x0, starting transfers between devices: 263 us -> none  [the longest x54 193 us: with_halo(): lax.ppermute(lax.slice_in_dim(block, block.shape[dim] - width, None, axis...]
    ppermute x108 -> x0, waiting for transfers between devices: 236 us -> none  [the longest x54 152 us: with_halo(): lax.ppermute(lax.slice_in_dim(block, 0, width, axis=dim), axis, backward)]
    pallas_call x0 -> x1, Pallas kernels: none -> 79.5 us  [shards(): pl.pallas_call(functools.partial(kernel, depth, kappa_table.shape[0]), ou...]
    reshape x16 -> x0, local copies, waits for them, and re-layouts: 78.9 us -> none  [the longest x8 72.4 us: coarsen_sum(): vector.reshape(shape[:-3] + (shape[-3] // 2, 2, shape[-2] // 2, 2, shape[...]
    psum x1 -> x0, blocking collectives: 44.5 us -> none  [shards(): lax.psum((local_rz, jnp.sum(direction * image, axis=(1, 2, 3))), ('gx', '...]
    reduce_sum x11 -> x0, other arithmetic: 29 us -> none  [the longest x10 28.4 us: coarsen_sum(): return jnp.sum(blocks, axis=(-5, -3, -1))]
    add x22 -> x0, other arithmetic: 25.4 us -> none  [the longest x17 11.2 us: smooth_pass(): approx = approx + weight * (source - operator(approx)) / coeffs[3]]
    mul x12 -> x0, other arithmetic: 23.4 us -> none  [the longest x1 11.4 us: shards(): vertical = look_up(classes, vertical_table) * sea]
  transfers between devices with their start and end apart: 108 -> 0, of which waited for: 70 -> 0; matrix products, arithmetic and copies ran while one was open for 8% -> 0% of each run, Pallas kernels for 0% -> 0%
where the time goes in v1:
time: 86.1 us; the launch traced here: 85.9 us
  Pallas kernels  79.5 us (92%)
  local copies, waits for them, and re-layouts  4.82 us (6%)
  other arithmetic  0.91 us (1%)
    pallas_call x1, Pallas kernels, shards(): pl.pallas_call(functools.partial(kernel, depth, kappa_table.shape[0]), ou...  79.5 us
    unnamed x12, local copies, waits for them, and re-layouts  4.71 us

profile of v1, /device:TPU:0, one launch (start us, length us, event | category | flops | bytes accessed | tf_op | source)
XLA Modules:
  0.0 85.9 jit_solution(4187474338732364529)
XLA Ops:
  0.6 0.0 copy-start
  0.6 0.9 %copy-done = f32[2,16,16,128]{3,2,1,0:T(8,128)S(1)} copy-done((f32[2,16,16,128]{3,2,1,0:T(8,128)S(1)}, f32[2,16,16,128]{3,2,1,0:T(8,128)}, u32[]{:S(2)}) %copy-start) | copy-done | bytes 262168
  1.6 0.0 copy-start.1
  1.6 0.9 %copy-done.1 = s32[16,16,128]{2,1,0:T(8,128)S(1)} copy-done((s32[16,16,128]{2,1,0:T(8,128)S(1)}, s32[16,16,128]{2,1,0:T(8,128)}, u32[]{:S(2)}) %copy-start.1) | copy-done | bytes 131096
  2.5 0.0 copy-start.2
  2.5 0.9 %copy-done.2 = s32[16,16,128]{2,1,0:T(8,128)S(1)} copy-done((s32[16,16,128]{2,1,0:T(8,128)S(1)}, s32[16,16,128]{2,1,0:T(8,128)}, u32[]{:S(2)}) %copy-start.2) | copy-done | bytes 131096
  3.4 0.0 copy-start.3
  3.4 0.7 copy-done.3
  4.0 0.0 copy-start.4
  4.0 0.7 copy-done.4
  4.7 0.0 copy-start.5
  4.7 0.7 copy-done.5
  5.4 79.5 %shard_map.77 = (f32[2,16,16,128]{3,2,1,0:T(8,128)S(1)}, f32[2,16,16,128]{3,2,1,0:T(8,128)S(1)}, f32[2,8,128]{2,1,0:T(8,128)S(1)}) custom-call(f32[2,16,16,128]{3,2,1,0:T(8,128)S(1)} %copy-done, s32[16,16,128]{2,1,0:T(8,128)S(1)} %copy-done.1, s32[16,16,128]{2,1,0:T(8,128)S(1)} %copy-done.2, f32[16]{0:T(128)S(1)} %copy-done.3, f32[16]{0:T(128)S(1)} %copy-done.4, ...), custom_call_target="tpu_custom_call" | custom-call | tf_op jit(solution)/shard_map/pallas_call | solution.py:442
  84.8 0.1 slice_reduce_fusion
  84.9 0.9 %multiply_subtract_fusion = (f32[2,16,16,128]{3,2,1,0:T(8,128)}, f32[2,16,16,128]{3,2,1,0:T(8,128)}) fusion(f32[2,16,16,128]{3,2,1,0:T(8,128)S(1)} %copy-done, f32[2,16,16,128]{3,2,1,0:T(8,128)S(1)} %get-tuple-element.7, f32[2]{0:T(128)S(1)} %slice_reduce_fusion, f32[2,16,16,128]{3,2,1,0:T(8,128)S(1)} %get-tuple-element.6), kind=kLoop, calls=%fused_computation | loop fusion | flops 196608 | bytes 1310728 | tf_op jit(solution)/shard_map/sub | solution.py:453
Async XLA Ops:
  0.6 1.0 %copy-start = (f32[2,16,16,128]{3,2,1,0:T(8,128)S(1)}, f32[2,16,16,128]{3,2,1,0:T(8,128)}, u32[]{:S(2)}) copy-start(f32[2,16,16,128]{3,2,1,0:T(8,128)} %refs_0_.1) | copy-start | bytes 786436
  1.6 0.9 %copy-start.1 = (s32[16,16,128]{2,1,0:T(8,128)S(1)}, s32[16,16,128]{2,1,0:T(8,128)}, u32[]{:S(2)}) copy-start(s32[16,16,128]{2,1,0:T(8,128)} %refs_1_.1) | copy-start | bytes 393220
  2.5 0.9 %copy-start.2 = (s32[16,16,128]{2,1,0:T(8,128)S(1)}, s32[16,16,128]{2,1,0:T(8,128)}, u32[]{:S(2)}) copy-start(s32[16,16,128]{2,1,0:T(8,128)} %refs_2_.1) | copy-start | bytes 393220
  3.4 0.7 copy-start.3
  4.0 0.7 copy-start.4
  4.7 0.7 copy-start.5

commit v2 on v1

--- a/solution.py
+++ b/solution.py
@@ -72,25 +72,54 @@
 
         loop(self.depth, body)
 
-    def operator(self, v, z):
-        x = v[:, z + 1]
+    def operators(self, v, z, count):
         step = self.step
-        total = self.fxm[z] * turn(x, step, 1) + self.fxp[z] * turn(x, -step, 1)
-        total = total + self.fym[z] * turn(x, step, 2) + self.fyp[z] * turn(x, -step, 2)
-        total = total + self.fz[z] * v[:, z] + self.fz[z + 1] * v[:, z + 2]
-        return self.d[z] * x - total
+        images = [[None, None] for _ in range(count)]
+        faces = [self.fz[z + i] for i in range(count + 1)]
+        for item in range(2):
+            planes = [v[item, z + i] for i in range(count + 2)]
+            for i in range(count):
+                x = planes[i + 1]
+                total = self.fxm[z + i] * turn(x, step, 0) + self.fxp[z + i] * turn(x, -step, 0)
+                total = total + self.fym[z + i] * turn(x, step, 1) + self.fyp[z + i] * turn(x, -step, 1)
+                total = total + faces[i] * planes[i] + faces[i + 1] * planes[i + 2]
+                images[i][item] = self.d[z + i] * x - total
+        return images
 
     def start(self, out, r, weight):
-        def body(z):
-            out[:, z + 1] = weight * r[:, z + 1] * self.inv[z]
-
-        loop(self.depth, body)
-
-    def smooth(self, out, v, r, weight):
-        def body(z):
-            out[:, z + 1] = v[:, z + 1] + weight * (r[:, z + 1] - self.operator(v, z)) * self.inv[z]
-
-        loop(self.depth, body)
+        def body(pair):
+            for i in range(2):
+                scale = weight * self.inv[2 * pair + i]
+                out[:, 2 * pair + i + 1] = r[:, 2 * pair + i + 1] * scale
+
+        loop(self.depth // 2, body)
+
+    def smooth(self, out, v, r, weight, own_only=False):
+        def body(pair):
+            z = 2 * pair
+            images = self.operators(v, z, 2)
+            fresh = []
+            for i in range(2):
+                scale = weight * self.inv[z + i]
+                for item in range(2):
+                    defect = r[item, z + i + 1] - images[i][item]
+                    fresh.append((item, i, v[item, z + i + 1] + scale * defect))
+            for item, i, value in fresh:
+                if own_only:
+                    out[item, z + i + 1, 0:ROWS, 0:LANES] = value[0:ROWS, 0:LANES]
+                else:
+                    out[item, z + i + 1] = value
+
+        loop(self.depth // 2, body)
+
+    def defect_sums(self, v, r, pair):
+        z = 2 * pair
+        images = self.operators(v, z, 2)
+        sums = []
+        for item in range(2):
+            q = (r[item, z + 1] - images[0][item]) + (r[item, z + 2] - images[1][item])
+            sums.append(pair_sum(q, self.step))
+        return sums
 
 
 class Exchange:
@@ -320,20 +349,20 @@
         level0.smooth(xb, xa, r, fine_w[1])
 
         def down0(z):
-            q = r[:, 2 * z + 1] - level0.operator(xb, 2 * z)
-            q = q + (r[:, 2 * z + 2] - level0.operator(xb, 2 * z + 1))
-            q = pair_sum(q, 1)
-            r1[:, z + 1] = q
-            ya[:, z + 1] = fine_w[0] * q * level1.inv[z]
+            sums = level0.defect_sums(xb, r, z)
+            scale = fine_w[0] * level1.inv[z]
+            for item in range(2):
+                r1[item, z + 1] = sums[item]
+                ya[item, z + 1] = sums[item] * scale
 
         loop(level1.depth, down0)
         level1.smooth(yb, ya, r1, fine_w[1])
         own2 = r2_own[turn_no]
 
         def down1(z):
-            q = r1[:, 2 * z + 1] - level1.operator(yb, 2 * z)
-            q = q + (r1[:, 2 * z + 2] - level1.operator(yb, 2 * z + 1))
-            own2[:, z] = pair_sum(q, 2)[:, 0:ROWS, 0:LANES]
+            sums = level1.defect_sums(yb, r1, z)
+            for item in range(2):
+                own2[item, z] = sums[item][0:ROWS, 0:LANES]
 
         loop(level2.depth, down1)
         e2 = ex[("e2a", "e2b")[turn_no]]
@@ -366,7 +395,7 @@
 
         loop(level2.depth, up1)
         level1.smooth(yb, ya, r1, fine_w[0])
-        level1.smooth(ya, yb, r1, fine_w[1])
+        level1.smooth(ya, yb, r1, fine_w[1], own_only=True)
         own = x_own[turn_no]
 
         def up0(z):
@@ -385,20 +414,29 @@
     cycle(r_first, r_second, 0)
     cycle(r_second, r_first, 1)
 
-    def first_image(z):
-        xb[:, z + 1] = level0.operator(r_first, z)
-
-    loop(depth, first_image)
-
-    def second_image(z, sums):
-        image = level0.operator(xb, z)[:, 0:ROWS, 0:LANES]
-        direction = r_first[:, z + 1, 0:ROWS, 0:LANES]
-        direction_out[:, z] = direction
-        image_out[:, z] = image
-        return sums[0] + right_side[:, z] * direction, sums[1] + direction * image
+    def first_image(pair):
+        images = level0.operators(r_first, 2 * pair, 2)
+        for i in range(2):
+            for item in range(2):
+                xb[item, 2 * pair + i + 1] = images[i][item]
+
+    loop(depth // 2, first_image)
+
+    def second_image(pair, sums):
+        rz, curve = sums
+        images = level0.operators(xb, 2 * pair, 2)
+        for i in range(2):
+            z = 2 * pair + i
+            image = jnp.stack([images[i][0][0:ROWS, 0:LANES], images[i][1][0:ROWS, 0:LANES]])
+            direction = r_first[:, z + 1, 0:ROWS, 0:LANES]
+            direction_out[:, z] = direction
+            image_out[:, z] = image
+            rz = rz + right_side[:, z] * direction
+            curve = curve + direction * image
+        return rz, curve
 
     zero = jnp.zeros((2, ROWS, LANES), jnp.float32)
-    rz, curve = lax.fori_loop(0, depth, second_image, (zero, zero))
+    rz, curve = lax.fori_loop(0, depth // 2, second_image, (zero, zero))
     part_x[0:2] = rz[:, 0:8] + rz[:, 8:16]
     part_x[2:4] = curve[:, 0:8] + curve[:, 8:16]
     part_y[...] = sum_over("gx", part_x, slots_x, sx_send, sx_recv)

time: 86.1 us -> 75.9 us (0.88)
  Pallas kernels: 79.5 us -> 69.3 us
    pallas_call x1, Pallas kernels: 79.5 us -> 69.3 us  [shards(): pl.pallas_call(functools.partial(kernel, depth, kappa_table.shape[0]), ou...]
where the time goes in v2:
time: 75.9 us; the launch traced here: 75.7 us
  Pallas kernels  69.3 us (91%)
  local copies, waits for them, and re-layouts  4.82 us (6%)
  other arithmetic  0.91 us (1%)
    pallas_call x1, Pallas kernels, shards(): pl.pallas_call(functools.partial(kernel, depth, kappa_table.shape[0]), ou...  69.3 us
    unnamed x12, local copies, waits for them, and re-layouts  4.71 us

profile of v2, /device:TPU:0, one launch (start us, length us, event | category | flops | bytes accessed | tf_op | source)
XLA Modules:
  0.0 75.7 jit_solution(17085788309543240780)
XLA Ops:
  0.6 0.0 copy-start
  0.6 0.9 %copy-done = f32[2,16,16,128]{3,2,1,0:T(8,128)S(1)} copy-done((f32[2,16,16,128]{3,2,1,0:T(8,128)S(1)}, f32[2,16,16,128]{3,2,1,0:T(8,128)}, u32[]{:S(2)}) %copy-start) | copy-done | bytes 262168
  1.6 0.0 copy-start.1
  1.6 0.9 %copy-done.1 = s32[16,16,128]{2,1,0:T(8,128)S(1)} copy-done((s32[16,16,128]{2,1,0:T(8,128)S(1)}, s32[16,16,128]{2,1,0:T(8,128)}, u32[]{:S(2)}) %copy-start.1) | copy-done | bytes 131096
  2.5 0.0 copy-start.2
  2.5 0.9 %copy-done.2 = s32[16,16,128]{2,1,0:T(8,128)S(1)} copy-done((s32[16,16,128]{2,1,0:T(8,128)S(1)}, s32[16,16,128]{2,1,0:T(8,128)}, u32[]{:S(2)}) %copy-start.2) | copy-done | bytes 131096
  3.4 0.0 copy-start.3
  3.4 0.7 copy-done.3
  4.0 0.0 copy-start.4
  4.0 0.7 copy-done.4
  4.7 0.0 copy-start.5
  4.7 0.7 copy-done.5
  5.4 69.3 %shard_map.77 = (f32[2,16,16,128]{3,2,1,0:T(8,128)S(1)}, f32[2,16,16,128]{3,2,1,0:T(8,128)S(1)}, f32[2,8,128]{2,1,0:T(8,128)S(1)}) custom-call(f32[2,16,16,128]{3,2,1,0:T(8,128)S(1)} %copy-done, s32[16,16,128]{2,1,0:T(8,128)S(1)} %copy-done.1, s32[16,16,128]{2,1,0:T(8,128)S(1)} %copy-done.2, f32[16]{0:T(128)S(1)} %copy-done.3, f32[16]{0:T(128)S(1)} %copy-done.4, ...), custom_call_target="tpu_custom_call" | custom-call | tf_op jit(solution)/shard_map/pallas_call | solution.py:480
  74.7 0.1 slice_reduce_fusion
  74.8 0.9 %multiply_subtract_fusion = (f32[2,16,16,128]{3,2,1,0:T(8,128)}, f32[2,16,16,128]{3,2,1,0:T(8,128)}) fusion(f32[2,16,16,128]{3,2,1,0:T(8,128)S(1)} %copy-done, f32[2,16,16,128]{3,2,1,0:T(8,128)S(1)} %get-tuple-element.7, f32[2]{0:T(128)S(1)} %slice_reduce_fusion, f32[2,16,16,128]{3,2,1,0:T(8,128)S(1)} %get-tuple-element.6), kind=kLoop, calls=%fused_computation | loop fusion | flops 196608 | bytes 1310728 | tf_op jit(solution)/shard_map/sub | solution.py:491
Async XLA Ops:
  0.6 1.0 %copy-start = (f32[2,16,16,128]{3,2,1,0:T(8,128)S(1)}, f32[2,16,16,128]{3,2,1,0:T(8,128)}, u32[]{:S(2)}) copy-start(f32[2,16,16,128]{3,2,1,0:T(8,128)} %refs_0_.1) | copy-start | bytes 786436
  1.6 0.9 %copy-start.1 = (s32[16,16,128]{2,1,0:T(8,128)S(1)}, s32[16,16,128]{2,1,0:T(8,128)}, u32[]{:S(2)}) copy-start(s32[16,16,128]{2,1,0:T(8,128)} %refs_1_.1) | copy-start | bytes 393220
  2.5 0.9 %copy-start.2 = (s32[16,16,128]{2,1,0:T(8,128)S(1)}, s32[16,16,128]{2,1,0:T(8,128)}, u32[]{:S(2)}) copy-start(s32[16,16,128]{2,1,0:T(8,128)} %refs_2_.1) | copy-start | bytes 393220
  3.4 0.7 copy-start.3
  4.0 0.7 copy-start.4
  4.7 0.7 copy-start.5

commit v3 on v2

--- a/solution.py
+++ b/solution.py
@@ -53,24 +53,26 @@
     def build(self, diagonal_known=False):
         step, factor = self.step, self.factor
 
-        def body(z):
-            w = self.w[z + 1]
-            fxp = factor * jnp.sqrt(w * turn(w, -step, 0))
-            fyp = factor * jnp.sqrt(w * turn(w, -step, 1))
-            fxm = turn(fxp, step, 0)
-            fym = turn(fyp, step, 1)
-            fzm = factor * jnp.sqrt(self.u[z] * self.u[z + 1])
-            fzp = factor * jnp.sqrt(self.u[z + 1] * self.u[z + 2])
-            d = self.k[z + 1]
-            if not diagonal_known:
-                d = d + fxm + fxp + fym + fyp + fzm + fzp
-            self.fxm[z], self.fxp[z], self.fym[z], self.fyp[z] = fxm, fxp, fym, fyp
-            self.fz[z] = fzm
-            self.fz[z + 1] = fzp
-            self.d[z] = d
-            self.inv[z] = jnp.where(d > 0.0, 1.0 / jnp.where(d > 0.0, d, 1.0), 0.0)
-
-        loop(self.depth, body)
+        def body(pair):
+            stores = []
+            for z in (2 * pair, 2 * pair + 1):
+                w = self.w[z + 1]
+                fxp = factor * jnp.sqrt(w * turn(w, -step, 0))
+                fyp = factor * jnp.sqrt(w * turn(w, -step, 1))
+                fxm = turn(fxp, step, 0)
+                fym = turn(fyp, step, 1)
+                fzm = factor * jnp.sqrt(self.u[z] * self.u[z + 1])
+                fzp = factor * jnp.sqrt(self.u[z + 1] * self.u[z + 2])
+                d = self.k[z + 1]
+                if not diagonal_known:
+                    d = d + fxm + fxp + fym + fyp + fzm + fzp
+                inv = jnp.where(d > 0.0, 1.0 / jnp.where(d > 0.0, d, 1.0), 0.0)
+                stores += [(self.fxm, z, fxm), (self.fxp, z, fxp), (self.fym, z, fym), (self.fyp, z, fyp)]
+                stores += [(self.fz, z, fzm), (self.fz, z + 1, fzp), (self.d, z, d), (self.inv, z, inv)]
+            for ref, z, value in stores:
+                ref[z] = value
+
+        loop(self.depth // 2, body)
 
     def operators(self, v, z, count):
         step = self.step
@@ -87,19 +89,19 @@
         return images
 
     def start(self, out, r, weight):
-        def body(pair):
-            for i in range(2):
-                scale = weight * self.inv[2 * pair + i]
-                out[:, 2 * pair + i + 1] = r[:, 2 * pair + i + 1] * scale
-
-        loop(self.depth // 2, body)
+        def body(group):
+            z = 4 * group
+            scale = weight * self.inv[pl.ds(z, 4)]
+            out[:, pl.ds(z + 1, 4)] = r[:, pl.ds(z + 1, 4)] * scale
+
+        loop(self.depth // 4, body)
 
     def smooth(self, out, v, r, weight, own_only=False):
-        def body(pair):
-            z = 2 * pair
-            images = self.operators(v, z, 2)
+        def body(group):
+            z = 4 * group
+            images = self.operators(v, z, 4)
             fresh = []
-            for i in range(2):
+            for i in range(4):
                 scale = weight * self.inv[z + i]
                 for item in range(2):
                     defect = r[item, z + i + 1] - images[i][item]
@@ -110,7 +112,7 @@
                 else:
                     out[item, z + i + 1] = value
 
-        loop(self.depth // 2, body)
+        loop(self.depth // 4, body)
 
     def defect_sums(self, v, r, pair):
         z = 2 * pair
@@ -288,9 +290,10 @@
 
     ex["r"].begin(right_side)
 
-    def look_up(z):
-        cls = classes[z]
-        sea = sea_mask[z].astype(jnp.float32)
+    def look_up(group):
+        four = pl.ds(4 * group, 4)
+        cls = classes[four]
+        sea = sea_mask[four].astype(jnp.float32)
         w = jnp.zeros(cls.shape, jnp.float32)
         u, k = w, w
         for entry in range(entries):
@@ -298,11 +301,11 @@
             w = jnp.where(here, cross[entry], w)
             u = jnp.where(here, vertical[entry], u)
             k = jnp.where(here, kappa[entry], k)
-        material[0, z] = w * sea
-        material[1, z] = u * sea
-        material[2, z] = k * sea + (1.0 - sea)
-
-    loop(depth, look_up)
+        material[0, four] = w * sea
+        material[1, four] = u * sea
+        material[2, four] = k * sea + (1.0 - sea)
+
+    loop(depth // 4, look_up)
     ex["mat"].begin(material)
     for ref in (r_first, r_second, xa, xb, r1, ya, yb, r2, za, zb):
         last = ref.shape[1] - 1
@@ -318,12 +321,11 @@
 
     def coarsen_material(fine, coarse, step):
         def body(z):
-            for src, dst, factor in (
-                (fine.w, coarse.w, 0.125),
-                (fine.u, coarse.u, 0.125),
-                (fine.k, coarse.k, 1.0),
-            ):
-                dst[z + 1] = factor * pair_sum(src[2 * z + 1] + src[2 * z + 2], step)
+            means = []
+            for src, factor in ((fine.w, 0.125), (fine.u, 0.125), (fine.k, 1.0)):
+                means.append(factor * pair_sum(src[2 * z + 1] + src[2 * z + 2], step))
+            for dst, value in zip((coarse.w, coarse.u, coarse.k), means):
+                dst[z + 1] = value
 
         loop(coarse.depth, body)
 

time: 75.9 us -> 70.4 us (0.928)
  Pallas kernels: 69.3 us -> 63.8 us
    pallas_call x1, Pallas kernels: 69.3 us -> 63.8 us  [shards(): pl.pallas_call(functools.partial(kernel, depth, kappa_table.shape[0]), ou...]
where the time goes in v3:
time: 70.4 us; the launch traced here: 70.1 us
  Pallas kernels  63.8 us (91%)
  local copies, waits for them, and re-layouts  4.82 us (7%)
  other arithmetic  0.91 us (1%)
    pallas_call x1, Pallas kernels, shards(): pl.pallas_call(functools.partial(kernel, depth, kappa_table.shape[0]), ou...  63.8 us
    unnamed x12, local copies, waits for them, and re-layouts  4.71 us

profile of v3, /device:TPU:0, one launch (start us, length us, event | category | flops | bytes accessed | tf_op | source)
XLA Modules:
  0.0 70.1 jit_solution(16795582849985995504)
XLA Ops:
  0.6 0.0 copy-start
  0.6 0.9 %copy-done = f32[2,16,16,128]{3,2,1,0:T(8,128)S(1)} copy-done((f32[2,16,16,128]{3,2,1,0:T(8,128)S(1)}, f32[2,16,16,128]{3,2,1,0:T(8,128)}, u32[]{:S(2)}) %copy-start) | copy-done | bytes 262168
  1.6 0.0 copy-start.1
  1.6 0.9 %copy-done.1 = s32[16,16,128]{2,1,0:T(8,128)S(1)} copy-done((s32[16,16,128]{2,1,0:T(8,128)S(1)}, s32[16,16,128]{2,1,0:T(8,128)}, u32[]{:S(2)}) %copy-start.1) | copy-done | bytes 131096
  2.5 0.0 copy-start.2
  2.5 0.9 %copy-done.2 = s32[16,16,128]{2,1,0:T(8,128)S(1)} copy-done((s32[16,16,128]{2,1,0:T(8,128)S(1)}, s32[16,16,128]{2,1,0:T(8,128)}, u32[]{:S(2)}) %copy-start.2) | copy-done | bytes 131096
  3.4 0.0 copy-start.3
  3.4 0.7 copy-done.3
  4.0 0.0 copy-start.4
  4.0 0.7 copy-done.4
  4.7 0.0 copy-start.5
  4.7 0.7 copy-done.5
  5.4 63.8 %shard_map.77 = (f32[2,16,16,128]{3,2,1,0:T(8,128)S(1)}, f32[2,16,16,128]{3,2,1,0:T(8,128)S(1)}, f32[2,8,128]{2,1,0:T(8,128)S(1)}) custom-call(f32[2,16,16,128]{3,2,1,0:T(8,128)S(1)} %copy-done, s32[16,16,128]{2,1,0:T(8,128)S(1)} %copy-done.1, s32[16,16,128]{2,1,0:T(8,128)S(1)} %copy-done.2, f32[16]{0:T(128)S(1)} %copy-done.3, f32[16]{0:T(128)S(1)} %copy-done.4, ...), custom_call_target="tpu_custom_call" | custom-call | tf_op jit(solution)/shard_map/pallas_call | solution.py:482
  69.1 0.1 slice_reduce_fusion
  69.2 0.9 %multiply_subtract_fusion = (f32[2,16,16,128]{3,2,1,0:T(8,128)}, f32[2,16,16,128]{3,2,1,0:T(8,128)}) fusion(f32[2,16,16,128]{3,2,1,0:T(8,128)S(1)} %copy-done, f32[2,16,16,128]{3,2,1,0:T(8,128)S(1)} %get-tuple-element.7, f32[2]{0:T(128)S(1)} %slice_reduce_fusion, f32[2,16,16,128]{3,2,1,0:T(8,128)S(1)} %get-tuple-element.6), kind=kLoop, calls=%fused_computation | loop fusion | flops 196608 | bytes 1310728 | tf_op jit(solution)/shard_map/sub | solution.py:493
Async XLA Ops:
  0.6 1.0 %copy-start = (f32[2,16,16,128]{3,2,1,0:T(8,128)S(1)}, f32[2,16,16,128]{3,2,1,0:T(8,128)}, u32[]{:S(2)}) copy-start(f32[2,16,16,128]{3,2,1,0:T(8,128)} %refs_0_.1) | copy-start | bytes 786436
  1.6 0.9 %copy-start.1 = (s32[16,16,128]{2,1,0:T(8,128)S(1)}, s32[16,16,128]{2,1,0:T(8,128)}, u32[]{:S(2)}) copy-start(s32[16,16,128]{2,1,0:T(8,128)} %refs_1_.1) | copy-start | bytes 393220
  2.5 0.9 %copy-start.2 = (s32[16,16,128]{2,1,0:T(8,128)S(1)}, s32[16,16,128]{2,1,0:T(8,128)}, u32[]{:S(2)}) copy-start(s32[16,16,128]{2,1,0:T(8,128)} %refs_2_.1) | copy-start | bytes 393220
  3.4 0.7 copy-start.3
  4.0 0.7 copy-start.4
  4.7 0.7 copy-start.5
